TPU v7x, 32 devices: a whole 2x2x4 slice. The times are simulated.
32 devices in a mesh: dp: 16 (over z, y, x), tensor: 2 (over core).
Axes of the slice: x: 2, y: 2, z: 4, core: 2. Of those that a mesh axis runs over, the one named last changes fastest.
Arguments:
- hidden_in: bfloat16 [512, 8192], P(None, 'tensor'), may hold values from -6 to 6
- teacher: bfloat16 [512, 8192], P(None, 'tensor'), may hold values from -3 to 3
- w_gate: bfloat16 [8192, 16384], P('tensor', 'dp'), may hold values from -0.0625 to 0.0625
- w_up: bfloat16 [8192, 16384], P('tensor', 'dp'), may hold values from -0.0625 to 0.0625
- w_down: bfloat16 [16384, 8192], P('dp', 'tensor'), may hold values from -0.046875 to 0.046875
- mask_gate: int32 [128, 256], P('tensor', 'dp'), may hold values 0 or 1
- mask_up: int32 [128, 256], P('tensor', 'dp'), may hold values 0 or 1
- mask_down: int32 [256, 128], P('dp', 'tensor'), may hold values 0 or 1
Outputs:
- grad_gate: bfloat16 [8192, 16384], P('tensor', 'dp')
- grad_up: bfloat16 [8192, 16384], P('tensor', 'dp')
- grad_down: bfloat16 [16384, 8192], P('dp', 'tensor')
All inputs are finite; a program needn't handle non-finite values. No bound on the sum of `mask_gate` or of `mask_up` or of `mask_down` on one device may be relied on, other than what follows from the above.
Results may differ from a plain program's by a relative error of at most 0.014.
Values may be sent and summed in bfloat16 or wider, within the bound.
A program may use at most 256 MiB of HBM per device.

v0:
```python
import jax
import jax.numpy as jnp
from jax import lax
from jax.sharding import PartitionSpec as P

BLOCK = 64


def widen(mask):
    return jnp.repeat(jnp.repeat(mask, BLOCK, axis=0), BLOCK, axis=1)


def contract_rows(left, right):
    return lax.dot_general(
        left, right, (((0,), (0,)), ((), ())), preferred_element_type=jnp.float32
    )


def contract_cols(left, right):
    return lax.dot_general(
        left, right, (((1,), (1,)), ((), ())), preferred_element_type=jnp.float32
    )


def on_device(hidden_in, teacher, w_gate, w_up, w_down, mask_gate, mask_up, mask_down):
    keep_gate = widen(mask_gate)
    keep_up = widen(mask_up)
    keep_down = widen(mask_down)
    sparse_gate = w_gate * keep_gate.astype(jnp.bfloat16)
    sparse_up = w_up * keep_up.astype(jnp.bfloat16)
    sparse_down = w_down * keep_down.astype(jnp.bfloat16)
    gate, up = lax.psum(
        (
            jnp.dot(hidden_in, sparse_gate, preferred_element_type=jnp.float32),
            jnp.dot(hidden_in, sparse_up, preferred_element_type=jnp.float32),
        ),
        "tensor",
    )
    sig = jax.nn.sigmoid(gate)
    act = gate * sig
    hidden_all = (act * up).astype(jnp.bfloat16)
    student = lax.psum(jnp.dot(hidden_all, sparse_down, preferred_element_type=jnp.float32), "dp")
    residual_all = (student - teacher.astype(jnp.float32)).astype(jnp.bfloat16)
    grad_down = (contract_rows(hidden_all, residual_all) * keep_down.astype(jnp.float32)).astype(
        jnp.bfloat16
    )
    grad_hidden = lax.psum(
        contract_cols(residual_all, sparse_down).astype(jnp.bfloat16), "tensor"
    ).astype(jnp.float32)
    grad_act_gate = (grad_hidden * up * sig * (1.0 + gate * (1.0 - sig))).astype(jnp.bfloat16)
    grad_act_up = (grad_hidden * act).astype(jnp.bfloat16)
    gate_total = contract_rows(hidden_in, grad_act_gate)
    up_total = contract_rows(hidden_in, grad_act_up)
    grad_gate = (gate_total * keep_gate.astype(jnp.float32)).astype(jnp.bfloat16)
    grad_up = (up_total * keep_up.astype(jnp.float32)).astype(jnp.bfloat16)
    return (grad_gate, grad_up, grad_down)


def solution(mesh):
    in_specs = (
        P(None, "tensor"),
        P(None, "tensor"),
        P("tensor", "dp"),
        P("tensor", "dp"),
        P("dp", "tensor"),
        P("tensor", "dp"),
        P("tensor", "dp"),
        P("dp", "tensor"),
    )
    out_specs = (P("tensor", "dp"), P("tensor", "dp"), P("dp", "tensor"))
    return jax.shard_map(
        on_device, mesh=mesh, in_specs=in_specs, out_specs=out_specs, check_vma=False
    )
```

profile of v0, /device:TPU:0, one launch (start us, length us, event | category | flops | bytes accessed | tf_op | source)
XLA Modules:
  0.0 452.9 jit_solution(12656934652470282091)
XLA Ops:
  7.2 0.8 fusion.14
  8.5 11.9 %copy.17 = bf16[4096,1024]{0,1:T(8,128)(2,1)} copy(bf16[4096,1024]{1,0:T(8,128)(2,1)} %param.11) | data formatting | bytes 16777216 | tf_op args[3]
  20.9 11.9 %copy.16 = bf16[4096,1024]{0,1:T(8,128)(2,1)} copy(bf16[4096,1024]{1,0:T(8,128)(2,1)} %param.10) | data formatting | bytes 16777216 | tf_op args[2]
  32.8 7.4 %bitcast_multiply_fusion.3 = bf16[4096,1024]{0,1:T(8,128)(2,1)} fusion(bf16[4096,1024]{0,1:T(8,128)(2,1)} %copy.17, bf16[4096,16]{0,1:T(8,128)(2,1)S(1)} %convert_element_type.100), kind=kLoop, calls=%fused_computation.6 | loop fusion | flops 4194304 | bytes 16908288 | tf_op jit(solution)/shard_map/mul | solution.py:30
  40.2 10.4 %convolution_bitcast_fusion = f32[512,1024]{0,1:T(8,128)} fusion(bf16[4096,1024]{0,1:T(8,128)(2,1)} %bitcast_multiply_fusion.3, bf16[512,4096]{1,0:T(8,128)(2,1)} %param.8), kind=kOutput, calls=%fused_computation.18 | convolution fusion | flops 4294967296 | bytes 14680064 | tf_op jit(solution)/shard_map/dot_general | solution.py:35
  50.6 7.4 %bitcast_multiply_fusion.4 = bf16[4096,1024]{0,1:T(8,128)(2,1)} fusion(bf16[4096,1024]{0,1:T(8,128)(2,1)} %copy.16, bf16[4096,16]{0,1:T(8,128)(2,1)S(1)} %convert_element_type.97), kind=kLoop, calls=%fused_computation.7 | loop fusion | flops 4194304 | bytes 16908288 | tf_op jit(solution)/shard_map/mul | solution.py:29
  58.0 10.4 %convolution_bitcast_fusion.1 = f32[512,1024]{0,1:T(8,128)} fusion(bf16[4096,1024]{0,1:T(8,128)(2,1)} %bitcast_multiply_fusion.4, bf16[512,4096]{1,0:T(8,128)(2,1)} %param.8), kind=kOutput, calls=%fused_computation.19 | convolution fusion | flops 4294967296 | bytes 14680064 | tf_op jit(solution)/shard_map/dot_general | solution.py:34
  68.7 0.4 copy-done.4
  69.6 12.1 %copy.19 = bf16[1024,4096]{0,1:T(8,128)(2,1)} copy(bf16[1024,4096]{1,0:T(8,128)(2,1)} %param.12) | data formatting | bytes 16777216 | tf_op args[4]
  81.8 7.6 %bitcast_multiply_fusion.2 = bf16[1024,4096]{0,1:T(8,128)(2,1)} fusion(bf16[1024,4096]{0,1:T(8,128)(2,1)} %copy.19, bf16[1024,64]{0,1:T(8,128)(2,1)S(1)} %convert_element_type.104), kind=kLoop, calls=%fused_computation.5 | loop fusion | flops 4194304 | bytes 16908288 | tf_op jit(solution)/shard_map/mul | solution.py:31
  89.3 10.5 %all-reduce.9.cloned.1.call-done = (f32[512,1024]{0,1:T(8,128)}, f32[512,1024]{0,1:T(8,128)}) async-done(((f32[512,1024]{0,1:T(8,128)}, f32[512,1024]{0,1:T(8,128)}), (f32[512,1024]{0,1:T(8,128)}, f32[512,1024]{0,1:T(8,128)})) %all-reduce.9.cloned.1.call-update) | async-done | bytes 4194320 | tf_op jit(solution)/shard_map/psum | solution.py:32
  99.9 2.9 multiply_convert_fusion.1
  102.7 10.3 %fusion.16 = f32[512,4096]{1,0:T(8,128)} fusion(bf16[512,1024]{0,1:T(8,128)(2,1)S(1)} %multiply_convert_fusion.1, bf16[1024,4096]{0,1:T(8,128)(2,1)} %bitcast_multiply_fusion.2), kind=kOutput, calls=%fused_computation.27 | convolution fusion | flops 4294967296 | bytes 17825792 | tf_op jit(solution)/shard_map/dot_general | solution.py:42
  114.0 8.8 %broadcast_in_dim.41 = f32[1024,64,64]{0,2,1:T(8,128)} broadcast(f32[1024,64]{0,1:T(8,128)S(1)} %convert_element_type.121), dimensions={0,1} | broadcast | bytes 17039360 | tf_op jit(solution)/shard_map/broadcast_in_dim | solution.py:10
  122.8 17.5 %copy.22 = f32[1024,4096]{1,0:T(8,128)} copy(f32[1024,4096]{0,1:T(8,128)} %bitcast.45) | data formatting | bytes 33554432 | tf_op jit(solution)/shard_map/convert_element_type | solution.py:44
  140.4 0.9 convert_element_type.117
  141.3 229.4 %all-reduce.5.cloned.1.call-done = f32[512,4096]{1,0:T(8,128)} async-done(((f32[512,4096]{1,0:T(8,128)}), f32[512,4096]{1,0:T(8,128)}) %all-reduce.5.cloned.1.call-update) | async-done | bytes 8388624 | tf_op jit(solution)/shard_map/psum | solution.py:42
  370.7 12.6 %convolution_convert_fusion = bf16[512,1024]{0,1:T(8,128)(2,1)} fusion(bf16[1024,4096]{0,1:T(8,128)(2,1)} %bitcast_multiply_fusion.2, f32[512,4096]{1,0:T(8,128)} %all-reduce.5.cloned.1.call-done, bf16[512,4096]{1,0:T(8,128)(2,1)} %param.9), kind=kOutput, calls=%fused_computation.20 | convolution fusion | flops 4301783040 | bytes 22020096 | tf_op jit(solution)/shard_map/dot_general | solution.py:20
  383.3 14.4 %multiply_convert_fusion = bf16[1024,4096]{1,0:T(8,128)(2,1)} fusion(f32[1024,4096]{1,0:T(8,128)} %copy.22, bf16[512,1024]{0,1:T(8,128)(2,1)S(1)} %multiply_convert_fusion.1, f32[512,4096]{1,0:T(8,128)} %all-reduce.5.cloned.1.call-done, bf16[512,4096]{1,0:T(8,128)(2,1)} %param.9), kind=kOutput, calls=%fused_computation.4 | convolution fusion | flops 4309647360 | bytes 38797312 | tf_op jit(solution)/shard_map/dot_general | solution.py:14
  397.7 4.2 all-reduce.7.cloned.1.call-done
  402.0 11.4 %fusion.1 = bf16[4096,1024]{0,1:T(8,128)(2,1)} fusion(bf16[512,4096]{1,0:T(8,128)(2,1)} %param.8, f32[4096,16]{0,1:T(8,128)S(1)} %convert_element_type.112, f32[512,1024]{0,1:T(8,128)} %get-tuple-element.9, bf16[512,1024]{0,1:T(8,128)(2,1)} %all-reduce.7.cloned.1.call-done, f32[512,1024]{0,1:T(8,128)S(1)} %copy-done), kind=kOutput, calls=%fused_computation.3 | convolution fusion | flops 4309123072 | bytes 18087936 | tf_op jit(solution)/shard_map/dot_general | solution.py:14
  413.4 12.0 %copy.23 = bf16[4096,1024]{1,0:T(8,128)(2,1)} copy(bf16[4096,1024]{0,1:T(8,128)(2,1)} %fusion.1) | data formatting | bytes 16777216
  425.5 9.0 %fusion = bf16[4096,1024]{0,1:T(8,128)(2,1)} fusion(bf16[512,4096]{1,0:T(8,128)(2,1)} %param.8, f32[4096,16]{0,1:T(8,128)S(1)} %copy-done.2, bf16[512,1024]{0,1:T(8,128)(2,1)S(1)} %copy-done.1, f32[512,1024]{0,1:T(8,128)S(1)} %copy-done), kind=kOutput, calls=%fused_computation.1 | convolution fusion | flops 4307025920 | bytes 15990784 | tf_op jit(solution)/shard_map/dot_general | solution.py:14
  434.4 11.9 %copy.24 = bf16[4096,1024]{1,0:T(8,128)(2,1)} copy(bf16[4096,1024]{0,1:T(8,128)(2,1)} %fusion) | data formatting | bytes 16777216
  (30 shorter events, 2.8 us)
Async XLA Ops:
  7.2 92.7 %all-reduce.9.cloned.1.call-start = ((), (), s32[]{:S(2)}) async-start(), calls=%async_computation.2 | async-start | bytes 8388608 | tf_op jit(solution)/shard_map/psum | solution.py:32
  8.5 11.9 %copy-start.3 = (s32[64,16]{0,1:T(8,128)S(1)}, s32[64,16]{0,1:T(8,128)}, u32[]{:S(2)}) copy-start(s32[64,16]{0,1:T(8,128)} %param.13) | copy-start | bytes 12292
  68.4 0.7 copy-start.4
  68.4 302.2 %all-reduce.5.cloned.1.call-start = ((), (), s32[]{:S(2)}) async-start(), calls=%async_computation | async-start | bytes 16777216 | tf_op jit(solution)/shard_map/psum | solution.py:42
  113.1 288.9 %all-reduce.7.cloned.1.call-start = ((), (), s32[]{:S(2)}) async-start(), calls=%async_computation.1 | async-start | bytes 2097152 | tf_op jit(solution)/shard_map/psum | solution.py:47
  383.3 18.7 %copy-start = (f32[512,1024]{0,1:T(8,128)S(1)}, f32[512,1024]{0,1:T(8,128)}, u32[]{:S(2)}) copy-start(f32[512,1024]{0,1:T(8,128)} %get-tuple-element.10) | copy-start | bytes 6291460
  413.4 12.0 %copy-start.1 = (bf16[512,1024]{0,1:T(8,128)(2,1)S(1)}, bf16[512,1024]{0,1:T(8,128)(2,1)}, u32[]{:S(2)}) copy-start(bf16[512,1024]{0,1:T(8,128)(2,1)} %all-reduce.7.cloned.1.call-done) | copy-start | bytes 3145732
  413.4 12.0 %copy-start.2 = (f32[4096,16]{0,1:T(8,128)S(1)}, f32[4096,16]{0,1:T(8,128)}, u32[]{:S(2)}) copy-start(f32[4096,16]{0,1:T(8,128)} %convert_element_type.117) | copy-start | bytes 786436
Sparse Core Ops, SparseCore 0:
  68.6 31.2 all-reduce.8
  113.2 257.4 all-reduce.4
  383.4 18.5 all-reduce.6
where the time goes:
time: 455 us; the launch traced here: 453 us
  waiting for transfers between devices  244 us (54%)
  local copies, waits for them, and re-layouts  90 us (20%)
  matrix products  78.6 us (17%)
  other arithmetic  26 us (6%)
  between operations  13.8 us (3%)
    psum x1, waiting for transfers between devices, on_device(): lax.psum(jnp.dot(hidden_all, sparse_down, preferred_element_type=jnp.floa...  229 us
    unnamed x15, local copies, waits for them, and re-layouts  60.4 us
    dot_general x3, matrix products, contract_rows(): lax.dot_general(left, right, (((0,), (0,)), ((), ())), preferred_element_...  34.8 us
    convert_element_type x3, local copies, waits for them, and re-layouts, on_device(): keep_down.astype(jnp.float32)  17.7 us
    dot_general x1, matrix products, contract_cols(): lax.dot_general(left, right, (((1,), (1,)), ((), ())), preferred_element_...  12.6 us
    psum x1, waiting for transfers between devices, on_device(): lax.psum((jnp.dot(hidden_in, sparse_gate, preferred_element_type=jnp.floa...  10.5 us
    dot_general x1, matrix products, on_device(): jnp.dot(hidden_in, sparse_gate, preferred_element_type=jnp.float32)  10.4 us
    dot_general x1, matrix products, on_device(): jnp.dot(hidden_in, sparse_up, preferred_element_type=jnp.float32)  10.4 us
  transfers between devices with their start and end apart: 3, of which 3 were waited for; matrix products, arithmetic and copies ran while one was open for 14% of the time, Pallas kernels for 0%

commit v1 on v0

--- a/solution.py
+++ b/solution.py
@@ -1,9 +1,15 @@
+import functools
+
 import jax
 import jax.numpy as jnp
 from jax import lax
+from jax.experimental import pallas as pl
+from jax.experimental.pallas import tpu as pltpu
 from jax.sharding import PartitionSpec as P
 
 BLOCK = 64
+TILE = 512
+VMEM = 56 * 1024 * 1024
 
 
 def widen(mask):
@@ -22,7 +28,7 @@
     )
 
 
-def on_device(hidden_in, teacher, w_gate, w_up, w_down, mask_gate, mask_up, mask_down):
+def plain(hidden_in, teacher, w_gate, w_up, w_down, mask_gate, mask_up, mask_down):
     keep_gate = widen(mask_gate)
     keep_up = widen(mask_up)
     keep_down = widen(mask_down)
@@ -56,6 +62,297 @@
     return (grad_gate, grad_up, grad_down)
 
 
+def masked(block, mask):
+    parts = [
+        block[i * BLOCK : (i + 1) * BLOCK] * mask[i : i + 1].astype(block.dtype)
+        for i in range(mask.shape[0])
+    ]
+    return jnp.concatenate(parts, axis=0)
+
+
+def activations(own_ref, peer_ref):
+    gate = own_ref[0] + peer_ref[0].astype(jnp.float32)
+    up = own_ref[1] + peer_ref[1].astype(jnp.float32)
+    sig = jax.nn.sigmoid(gate)
+    return gate, up, sig, gate * sig
+
+
+def forward_kernel(x_ref, wg_ref, wu_ref, mg_ref, mu_ref, own_ref, send_ref):
+    k = pl.program_id(0)
+    for i, (w_ref, m_ref) in enumerate(((wg_ref, mg_ref), (wu_ref, mu_ref))):
+        part = jnp.dot(
+            x_ref[...], masked(w_ref[...], m_ref[...]), preferred_element_type=jnp.float32
+        )
+
+        @pl.when(k == 0)
+        def _():
+            own_ref[i] = part
+
+        @pl.when(k > 0)
+        def _():
+            own_ref[i] += part
+
+    @pl.when(k == pl.num_programs(0) - 1)
+    def _():
+        send_ref[...] = own_ref[...].astype(jnp.bfloat16)
+
+
+def student_kernel(own_ref, peer_ref, wd_ref, md_ref, part_ref, hidden_ref):
+    @pl.when(pl.program_id(0) == 0)
+    def _():
+        _, up, _, act = activations(own_ref, peer_ref)
+        hidden_ref[...] = (act * up).astype(jnp.bfloat16)
+
+    part_ref[0] = jnp.dot(
+        hidden_ref[...], masked(wd_ref[...], md_ref[...]), preferred_element_type=jnp.float32
+    ).astype(jnp.bfloat16)
+
+
+def residual_kernel(n, part_ref, teacher_ref, out_ref, acc, recv, teach, tsem, ssem, rsem):
+    groups, tokens, width = part_ref.shape
+    me = lax.axis_index("dp")
+    bits = n.bit_length() - 1
+    up = list(range(bits))
+    swap = [1, 0] + up[2:]
+    far = up[2:] + up[:2]
+    orders = [(up, swap, far, up, swap, up, swap, far)[g % 8] for g in range(groups)]
+
+    def partner(b):
+        return me + (1 - 2 * (lax.rem(me // 2**b, 2))) * 2**b
+
+    barrier = pltpu.get_barrier_semaphore()
+    for b in range(bits):
+        pl.semaphore_signal(
+            barrier, inc=1, device_id={"dp": partner(b)}, device_id_type=pl.DeviceIdType.MESH
+        )
+    pl.semaphore_wait(barrier, bits)
+
+    def at(start, rows):
+        return pl.ds(pl.multiple_of(start, rows), rows)
+
+    copies = []
+
+    def send(g, step, b, src, dst):
+        copy = pltpu.make_async_remote_copy(
+            src_ref=src,
+            dst_ref=dst,
+            send_sem=ssem.at[g, step],
+            recv_sem=rsem.at[g, step],
+            device_id={"dp": partner(b)},
+            device_id_type=pl.DeviceIdType.MESH,
+        )
+        copy.start()
+        copies.append(copy)
+        return copy
+
+    starts = [[0] for _ in range(groups)]
+    for g in range(groups):
+        for s in range(bits):
+            bit = lax.rem(me // 2 ** orders[g][s], 2)
+            starts[g].append(starts[g][s] + bit * (tokens >> (s + 1)))
+
+    def offset(s):
+        return tokens - (tokens >> s)
+
+    def halves(g, s):
+        half = tokens >> (s + 1)
+        bit = lax.rem(me // 2 ** orders[g][s], 2)
+        base = 0 if s == 0 else offset(s - 1)
+        src = part_ref if s == 0 else acc
+        return (
+            src.at[g, at(base + bit * half, half)],
+            src.at[g, at(base + (1 - bit) * half, half)],
+        )
+
+    def scatter(g, s):
+        half = tokens >> (s + 1)
+        return send(
+            g, s, orders[g][s], halves(g, s)[1], recv.at[g, pl.ds(offset(s), half)]
+        )
+
+    last = tokens >> bits
+    pending = [scatter(g, 0) for g in range(groups)]
+    teachers = []
+    for g in range(groups):
+        copy = pltpu.make_async_copy(
+            teacher_ref.at[at(starts[g][bits], last), pl.ds(g * width, width)],
+            teach.at[g],
+            tsem.at[g],
+        )
+        copy.start()
+        teachers.append(copy)
+
+    for s in range(bits):
+        half = tokens >> (s + 1)
+        for g in range(groups):
+            pending[g].wait_recv()
+            kept = halves(g, s)[0][...].astype(jnp.float32)
+            total = kept + recv[g, pl.ds(offset(s), half)].astype(jnp.float32)
+            if s < bits - 1:
+                acc[g, pl.ds(offset(s), half)] = total.astype(jnp.bfloat16)
+                pending[g] = scatter(g, s + 1)
+            else:
+                teachers[g].wait()
+                rows = at(starts[g][bits], last)
+                out_ref[g, rows] = (total - teach[g].astype(jnp.float32)).astype(jnp.bfloat16)
+                here = out_ref.at[g, rows]
+                pending[g] = send(g, bits, orders[g][s], here, here)
+    for t in range(1, bits + 1):
+        for g in range(groups):
+            pending[g].wait_recv()
+            if t < bits:
+                s = bits - 1 - t
+                here = out_ref.at[g, at(starts[g][s + 1], tokens >> (s + 1))]
+                pending[g] = send(g, bits + t, orders[g][s], here, here)
+    for copy in copies:
+        copy.wait_send()
+
+
+def down_kernel(res_ref, hidden_ref, wd_ref, md_ref, gd_ref, gh_ref, send_ref, turned):
+    k = pl.program_id(0)
+
+    @pl.when(k == 0)
+    def _():
+        turned[...] = hidden_ref[...].T
+
+    res = res_ref[0]
+    mask = md_ref[...]
+    gd = jnp.dot(turned[...], res, preferred_element_type=jnp.float32)
+    gd_ref[...] = masked(gd, mask).astype(jnp.bfloat16)
+    gh = contract_cols(res, masked(wd_ref[...], mask))
+
+    @pl.when(k == 0)
+    def _():
+        gh_ref[...] = gh
+
+    @pl.when(k > 0)
+    def _():
+        gh_ref[...] += gh
+
+    @pl.when(k == pl.num_programs(0) - 1)
+    def _():
+        send_ref[...] = gh_ref[...].astype(jnp.bfloat16)
+
+
+def weights_kernel(
+    own_ref, peer_ref, gh_ref, gh_peer_ref, x_ref, mg_ref, mu_ref, gg_ref, gu_ref, grads
+):
+    hidden = gg_ref.shape[1]
+
+    @pl.when(pl.program_id(0) == 0)
+    def _():
+        gate, up, sig, act = activations(own_ref, peer_ref)
+        gh = gh_ref[...] + gh_peer_ref[...].astype(jnp.float32)
+        grads[:, :hidden] = (gh * up * sig * (1.0 + gate * (1.0 - sig))).astype(jnp.bfloat16)
+        grads[:, hidden:] = (gh * act).astype(jnp.bfloat16)
+
+    turned = x_ref[...].T
+    for i, (m_ref, out_ref) in enumerate(((mg_ref, gg_ref), (mu_ref, gu_ref))):
+        total = jnp.dot(
+            turned, grads[:, i * hidden : (i + 1) * hidden], preferred_element_type=jnp.float32
+        )
+        out_ref[...] = masked(total, m_ref[...]).astype(jnp.bfloat16)
+
+
+def params(**more):
+    return pltpu.CompilerParams(vmem_limit_bytes=VMEM, **more)
+
+
+def whole(shape):
+    return pl.BlockSpec(shape, lambda k: (0,) * len(shape))
+
+
+def with_kernels(n, hidden_in, teacher, w_gate, w_up, w_down, mask_gate, mask_up, mask_down):
+    tokens, depth = hidden_in.shape
+    units = w_gate.shape[1]
+    tile = TILE
+    steps = depth // tile
+    f32, bf16 = jnp.float32, jnp.bfloat16
+    rows = tile // BLOCK
+    shape = jax.ShapeDtypeStruct
+    wide_gate = jnp.repeat(mask_gate.astype(f32), BLOCK, axis=1)
+    wide_up = jnp.repeat(mask_up.astype(f32), BLOCK, axis=1)
+    wide_down = jnp.repeat(mask_down.astype(f32), BLOCK, axis=1)
+    x_spec = pl.BlockSpec((tokens, tile), lambda k: (0, k))
+    w_spec = pl.BlockSpec((tile, units), lambda k: (k, 0))
+    m_spec = pl.BlockSpec((rows, units), lambda k: (k, 0))
+    wd_spec = pl.BlockSpec((units, tile), lambda k: (0, k))
+    md_spec = pl.BlockSpec((units // BLOCK, tile), lambda k: (0, k))
+    part_spec = pl.BlockSpec((1, tokens, tile), lambda k: (k, 0, 0))
+    both, one = (2, tokens, units), (tokens, units)
+    product = 2 * tokens * depth * units
+
+    def cost(products, moved):
+        return pl.CostEstimate(flops=products * product, bytes_accessed=moved, transcendentals=0)
+
+    own, mine = pl.pallas_call(
+        forward_kernel,
+        grid=(steps,),
+        in_specs=[x_spec, w_spec, w_spec, m_spec, m_spec],
+        out_specs=[whole(both), whole(both)],
+        out_shape=[shape(both, f32), shape(both, bf16)],
+        compiler_params=params(),
+        cost_estimate=cost(2, 4 * depth * units),
+    )(hidden_in, w_gate, w_up, wide_gate, wide_up)
+    peer = lax.ppermute(mine, "tensor", [(0, 1), (1, 0)])
+    partial, hidden = pl.pallas_call(
+        student_kernel,
+        grid=(steps,),
+        in_specs=[whole(both), whole(both), wd_spec, md_spec],
+        out_specs=[part_spec, whole(one)],
+        out_shape=[shape((steps, tokens, tile), bf16), shape(one, bf16)],
+        compiler_params=params(),
+        cost_estimate=cost(1, 2 * depth * units),
+    )(own, peer, w_down, wide_down)
+    bits = n.bit_length() - 1
+    residual = pl.pallas_call(
+        functools.partial(residual_kernel, n),
+        in_specs=[pl.BlockSpec(memory_space=pltpu.VMEM), pl.BlockSpec(memory_space=pl.ANY)],
+        out_specs=pl.BlockSpec(memory_space=pltpu.VMEM),
+        out_shape=shape((steps, tokens, tile), bf16),
+        scratch_shapes=[
+            pltpu.VMEM((steps, tokens, tile), bf16),
+            pltpu.VMEM((steps, tokens, tile), bf16),
+            pltpu.VMEM((steps, tokens // n, tile), bf16),
+            pltpu.SemaphoreType.DMA((steps,)),
+            pltpu.SemaphoreType.DMA((steps, 2 * bits)),
+            pltpu.SemaphoreType.DMA((steps, 2 * bits)),
+        ],
+        compiler_params=params(collective_id=0, has_side_effects=True),
+    )(partial, teacher)
+    grad_down, gh, gh_mine = pl.pallas_call(
+        down_kernel,
+        grid=(steps,),
+        in_specs=[part_spec, whole(one), wd_spec, md_spec],
+        out_specs=[wd_spec, whole(one), whole(one)],
+        out_shape=[shape((units, depth), bf16), shape(one, f32), shape(one, bf16)],
+        scratch_shapes=[pltpu.VMEM((units, tokens), bf16)],
+        compiler_params=params(),
+        cost_estimate=cost(2, 4 * depth * units),
+    )(residual, hidden, w_down, wide_down)
+    gh_peer = lax.ppermute(gh_mine, "tensor", [(0, 1), (1, 0)])
+    grad_gate, grad_up = pl.pallas_call(
+        weights_kernel,
+        grid=(steps,),
+        in_specs=[whole(both), whole(both), whole(one), whole(one), x_spec, m_spec, m_spec],
+        out_specs=[w_spec, w_spec],
+        out_shape=[shape((depth, units), bf16)] * 2,
+        scratch_shapes=[pltpu.VMEM((tokens, 2 * units), bf16)],
+        compiler_params=params(),
+        cost_estimate=cost(2, 4 * depth * units),
+    )(own, peer, gh, gh_peer, hidden_in, wide_gate, wide_up)
+    return (grad_gate, grad_up, grad_down)
+
+
+def on_device(n, tensor, *args):
+    tokens, depth = args[0].shape
+    units = args[2].shape[1]
+    fits = tensor == 2 and n >= 4 and n & (n - 1) == 0 and tokens % (16 * n) == 0
+    if fits and depth % TILE == 0 and units % 256 == 0:
+        return with_kernels(n, *args)
+    return plain(*args)
+
+
 def solution(mesh):
     in_specs = (
         P(None, "tensor"),
@@ -69,5 +366,7 @@
     )
     out_specs = (P("tensor", "dp"), P("tensor", "dp"), P("dp", "tensor"))
     return jax.shard_map(
-        on_device, mesh=mesh, in_specs=in_specs, out_specs=out_specs, check_vma=False
-    )
+        functools.partial(on_device, mesh.shape["dp"], mesh.shape["tensor"]),
+        mesh=mesh,
+         in_specs=in_specs, out_specs=out_specs, check_vma=False
+    )

time: 455 us -> 168 us (0.37)
  waiting for transfers between devices: 244 us -> 5.75 us
  Pallas kernels: 0 us -> 153 us
  local copies, waits for them, and re-layouts: 90 us -> 5.77 us
  matrix products: 78.6 us -> 0 us
  other arithmetic: 26 us -> 1.4 us
  between operations: 13.8 us -> 0.68 us
    psum x3 -> x0, waiting for transfers between devices: 244 us -> none  [the longest x1 229 us: on_device(): lax.psum(jnp.dot(hidden_all, sparse_down, preferred_element_type=jnp.floa...]
    pallas_call x0 -> x5, Pallas kernels: none -> 153 us  [the longest x1 86.7 us: with_kernels(): pl.pallas_call(functools.partial(residual_kernel, n), in_specs=[pl.BlockS...]
    dot_general x7 -> x0, matrix products: 78.6 us -> none  [the longest x3 34.8 us: contract_rows(): lax.dot_general(left, right, (((0,), (0,)), ((), ())), preferred_element_...]
    unnamed x15 -> x6, local copies, waits for them, and re-layouts: 60.4 us -> 2.33 us
    mul x3 -> x0, other arithmetic: 22.4 us -> none  [the longest x1 7.58 us: on_device(): sparse_down = w_down * keep_down.astype(jnp.bfloat16)]
    convert_element_type x9 -> x2, local copies, waits for them, and re-layouts: 19.7 us -> 0.17 us  [the longest x1 0.09 us: with_kernels(): wide_up = jnp.repeat(mask_up.astype(f32), BLOCK, axis=1)]
    broadcast_in_dim x7 -> x3, local copies, waits for them, and re-layouts: 9.94 us -> 0.57 us  [the longest x1 0.19 us: with_kernels(): wide_down = jnp.repeat(mask_down.astype(f32), BLOCK, axis=1)]
    ppermute x0 -> x2, waiting for transfers between devices: none -> 5.75 us  [the longest x1 2.89 us: with_kernels(): peer = lax.ppermute(mine, 'tensor', [(0, 1), (1, 0)])]
  transfers between devices with their start and end apart: 3 -> 2, of which waited for: 3 -> 2; matrix products, arithmetic and copies ran while one was open for 14% -> 1% of each run, Pallas kernels for 0% -> 0%
where the time goes in v1:
time: 168 us; the launch traced here: 167 us
  Pallas kernels  153 us (91%)
  local copies, waits for them, and re-layouts  5.77 us (3%)
  waiting for transfers between devices  5.75 us (3%)
    pallas_call x1, Pallas kernels, with_kernels(): pl.pallas_call(functools.partial(residual_kernel, n), in_specs=[pl.BlockS...  86.7 us
    pallas_call x1, Pallas kernels, with_kernels(): pl.pallas_call(forward_kernel, grid=(steps,), in_specs=[x_spec, w_spec, w...  19.3 us
    pallas_call x1, Pallas kernels, with_kernels(): pl.pallas_call(down_kernel, grid=(steps,), in_specs=[part_spec, whole(one...  17.1 us
    pallas_call x1, Pallas kernels, with_kernels(): pl.pallas_call(weights_kernel, grid=(steps,), in_specs=[whole(both), whol...  16.9 us
    pallas_call x1, Pallas kernels, with_kernels(): pl.pallas_call(student_kernel, grid=(steps,), in_specs=[whole(both), whol...  12.7 us
  transfers between devices with their start and end apart: 2, of which 2 were waited for; matrix products, arithmetic and copies ran while one was open for 1% of the time, Pallas kernels for 0%

profile of v1, /device:TPU:0, one launch (start us, length us, event | category | flops | bytes accessed | tf_op | source)
XLA Modules:
  0.0 166.9 jit_solution(1831268313481477269)
XLA Ops:
  0.6 0.7 convert_element_type.9
  1.3 0.7 convert_element_type.10
  2.0 0.1 copy.12
  2.1 0.1 copy.11
  2.2 0.2 broadcast_in_dim.9
  2.4 0.9 reshape.15.mg_ref
  3.3 0.2 broadcast_in_dim.10
  3.5 0.9 reshape.16.mu_ref
  4.4 0.0 copy-start
  4.4 19.3 %shard_map.103 = (f32[2,512,1024]{2,1,0:T(8,128)}, bf16[2,512,1024]{2,1,0:T(8,128)(2,1)}) custom-call(bf16[512,4096]{1,0:T(8,128)(2,1)} %x_ref.3, bf16[4096,1024]{1,0:T(8,128)(2,1)} %wg_ref.1, bf16[4096,1024]{1,0:T(8,128)(2,1)} %wu_ref.1, f32[64,1024]{1,0:T(8,128)} %reshape.15.mg_ref, f32[64,1024]{1,0:T(8,128)} %reshape.16.mu_ref), custom_call_target="tpu_custom_call" | custom-call | flops 8589934592 | bytes 16777216 | tf_op jit(solution)/shard_map/pallas_call | solution.py:288
  23.7 0.5 collective-permute-start
  24.1 0.0 copy-done
  24.2 0.2 broadcast_in_dim.11
  24.4 0.9 reshape.17.md_ref
  25.3 2.9 %collective-permute-done.peer_ref = bf16[2,512,1024]{2,1,0:T(8,128)(2,1)S(1)} collective-permute-done((bf16[2,512,1024]{2,1,0:T(8,128)(2,1)}, bf16[2,512,1024]{2,1,0:T(8,128)(2,1)S(1)}, u32[]{:S(2)}, u32[]{:S(2)}) %collective-permute-start) | collective-permute-done | bytes 2097184 | tf_op jit(solution)/shard_map/ppermute | solution.py:297
  28.1 0.0 copy-start.1
  28.1 1.4 copy-done.1
  29.5 12.7 %shard_map.104 = (bf16[8,512,512]{2,1,0:T(8,128)(2,1)}, bf16[512,1024]{1,0:T(8,128)(2,1)}) custom-call(f32[2,512,1024]{2,1,0:T(8,128)} %get-tuple-element.12.own_ref, bf16[2,512,1024]{2,1,0:T(8,128)(2,1)} %copy-done.1, bf16[1024,4096]{1,0:T(8,128)(2,1)} %wd_ref.3, f32[16,4096]{1,0:T(8,128)} %reshape.17.md_ref), custom_call_target="tpu_custom_call" | custom-call | flops 4294967296 | bytes 8388608 | tf_op jit(solution)/shard_map/pallas_call | solution.py:298
  42.3 86.7 %shard_map.105.res_ref = bf16[8,512,512]{2,1,0:T(8,128)(2,1)} custom-call(bf16[8,512,512]{2,1,0:T(8,128)(2,1)} %get-tuple-element.14.part_ref, bf16[512,4096]{1,0:T(8,128)(2,1)} %teacher_ref.1), custom_call_target="tpu_custom_call" | custom-call | tf_op jit(solution)/shard_map/pallas_call | solution.py:308
  128.9 17.1 %shard_map.106 = (bf16[1024,4096]{1,0:T(8,128)(2,1)}, f32[512,1024]{1,0:T(8,128)}, bf16[512,1024]{1,0:T(8,128)(2,1)}) custom-call(bf16[8,512,512]{2,1,0:T(8,128)(2,1)} %shard_map.105.res_ref, bf16[512,1024]{1,0:T(8,128)(2,1)} %get-tuple-element.15.hidden_ref, bf16[1024,4096]{1,0:T(8,128)(2,1)} %wd_ref.3, f32[16,4096]{1,0:T(8,128)} %reshape.17.md_ref), custom_call_target="tpu_custom_call" | custom-call | flops 8589934592 | bytes 16777216 | tf_op jit(solution)/shard_map/pallas_call | solution.py:323
  146.1 0.0 collective-permute-start.1
  146.1 2.9 %collective-permute-done.1.gh_peer_ref = bf16[512,1024]{1,0:T(8,128)(2,1)S(1)} collective-permute-done((bf16[512,1024]{1,0:T(8,128)(2,1)}, bf16[512,1024]{1,0:T(8,128)(2,1)S(1)}, u32[]{:S(2)}, u32[]{:S(2)}) %collective-permute-start.1) | collective-permute-done | bytes 1048608 | tf_op jit(solution)/shard_map/ppermute | solution.py:333
  149.0 1.0 copy-done.2
  149.9 16.9 %shard_map.107 = (bf16[4096,1024]{1,0:T(8,128)(2,1)}, bf16[4096,1024]{1,0:T(8,128)(2,1)}) custom-call(f32[2,512,1024]{2,1,0:T(8,128)} %get-tuple-element.12.own_ref, bf16[2,512,1024]{2,1,0:T(8,128)(2,1)} %copy-done.1, f32[512,1024]{1,0:T(8,128)} %get-tuple-element.16.gh_ref, bf16[512,1024]{1,0:T(8,128)(2,1)} %copy-done.2, bf16[512,4096]{1,0:T(8,128)(2,1)} %x_ref.3, ...), custom_call_target="tpu_custom_call" | custom-call | flops 8589934592 | bytes 16777216 | tf_op jit(solution)/shard_map/pallas_call | solution.py:334
  (2 shorter events, 0.0 us)
Async XLA Ops:
  4.4 19.8 %copy-start = (s32[16,64]{1,0:T(8,128)S(1)}, s32[16,64]{1,0:T(8,128)}, u32[]{:S(2)}) copy-start(s32[16,64]{1,0:T(8,128)} %param.15) | copy-start | bytes 12292
  23.7 4.5 %collective-permute-start = (bf16[2,512,1024]{2,1,0:T(8,128)(2,1)}, bf16[2,512,1024]{2,1,0:T(8,128)(2,1)S(1)}, u32[]{:S(2)}, u32[]{:S(2)}) collective-permute-start(bf16[2,512,1024]{2,1,0:T(8,128)(2,1)} %get-tuple-element.13), channel_id=1, source_target_pairs={{0,1},{1,0},{2,3},{3,2},{4,5},{5,4},{6,7},{7,6},{8,9},{9,8},{10,11... | collective-permute-start | bytes 6291464 | tf_op jit(solution)/shard_map/ppermute | solution.py:297
  28.1 1.4 copy-start.1
  146.1 2.9 %collective-permute-start.1 = (bf16[512,1024]{1,0:T(8,128)(2,1)}, bf16[512,1024]{1,0:T(8,128)(2,1)S(1)}, u32[]{:S(2)}, u32[]{:S(2)}) collective-permute-start(bf16[512,1024]{1,0:T(8,128)(2,1)} %get-tuple-element.17), channel_id=1, source_target_pairs={{0,1},{1,0},{2,3},{3,2},{4,5},{5,4},{6,7},{7,6},{8,9},{9,8},{10,11... | collective-permute-start | bytes 3145736 | tf_op jit(solution)/shard_map/ppermute | solution.py:333
  149.0 1.0 copy-start.2

commit v2 on v1

--- a/solution.py
+++ b/solution.py
@@ -70,6 +70,15 @@
     return jnp.concatenate(parts, axis=0)
 
 
+def widened(mask, first, width):
+    shape = (mask.shape[1], width)
+    column = lax.div(lax.broadcasted_iota(jnp.int32, shape, 1), BLOCK) + first
+    pick = (lax.broadcasted_iota(jnp.int32, shape, 0) == column).astype(jnp.bfloat16)
+    return jnp.dot(
+        mask.astype(jnp.float32).astype(jnp.bfloat16), pick, preferred_element_type=jnp.float32
+    )
+
+
 def activations(own_ref, peer_ref):
     gate = own_ref[0] + peer_ref[0].astype(jnp.float32)
     up = own_ref[1] + peer_ref[1].astype(jnp.float32)
@@ -80,8 +89,9 @@
 def forward_kernel(x_ref, wg_ref, wu_ref, mg_ref, mu_ref, own_ref, send_ref):
     k = pl.program_id(0)
     for i, (w_ref, m_ref) in enumerate(((wg_ref, mg_ref), (wu_ref, mu_ref))):
+        mask = widened(m_ref[...], 0, w_ref.shape[1])
         part = jnp.dot(
-            x_ref[...], masked(w_ref[...], m_ref[...]), preferred_element_type=jnp.float32
+            x_ref[...], masked(w_ref[...], mask), preferred_element_type=jnp.float32
         )
 
         @pl.when(k == 0)
@@ -97,25 +107,43 @@
         send_ref[...] = own_ref[...].astype(jnp.bfloat16)
 
 
-def student_kernel(own_ref, peer_ref, wd_ref, md_ref, part_ref, hidden_ref):
-    @pl.when(pl.program_id(0) == 0)
-    def _():
-        _, up, _, act = activations(own_ref, peer_ref)
-        hidden_ref[...] = (act * up).astype(jnp.bfloat16)
-
-    part_ref[0] = jnp.dot(
-        hidden_ref[...], masked(wd_ref[...], md_ref[...]), preferred_element_type=jnp.float32
-    ).astype(jnp.bfloat16)
-
-
-def residual_kernel(n, part_ref, teacher_ref, out_ref, acc, recv, teach, tsem, ssem, rsem):
+def residual_kernel(
+    n,
+    own_ref,
+    peer_ref,
+    md_ref,
+    wd_ref,
+    teacher_ref,
+    out_ref,
+    turned_ref,
+    factors_ref,
+    gh_ref,
+    gh_send_ref,
+    hidden,
+    part_ref,
+    sparse,
+    acc,
+    recv,
+    teach,
+    wsem,
+    tsem,
+    ssem,
+    rsem,
+):
     groups, tokens, width = part_ref.shape
+    weights = []
+    for g in range(groups):
+        copy = pltpu.make_async_copy(
+            wd_ref.at[:, pl.ds(g * width, width)], sparse.at[g], wsem.at[g]
+        )
+        copy.start()
+        weights.append(copy)
     me = lax.axis_index("dp")
     bits = n.bit_length() - 1
-    up = list(range(bits))
-    swap = [1, 0] + up[2:]
-    far = up[2:] + up[:2]
-    orders = [(up, swap, far, up, swap, up, swap, far)[g % 8] for g in range(groups)]
+    near = list(range(bits))
+    swap = [1, 0] + near[2:]
+    far = near[2:] + near[:2]
+    orders = [(near, swap, far, near, swap, near, swap, far)[g % 8] for g in range(groups)]
 
     def partner(b):
         return me + (1 - 2 * (lax.rem(me // 2**b, 2))) * 2**b
@@ -125,6 +153,8 @@
         pl.semaphore_signal(
             barrier, inc=1, device_id={"dp": partner(b)}, device_id_type=pl.DeviceIdType.MESH
         )
+    _, up_sum, _, act = activations(own_ref, peer_ref)
+    hidden[...] = (act * up_sum).astype(jnp.bfloat16)
     pl.semaphore_wait(barrier, bits)
 
     def at(start, rows):
@@ -171,7 +201,15 @@
         )
 
     last = tokens >> bits
-    pending = [scatter(g, 0) for g in range(groups)]
+    pending = []
+    for g in range(groups):
+        weights[g].wait()
+        mask = widened(md_ref[...], g * (width // BLOCK), width)
+        sparse[g] = masked(sparse[g], mask)
+        part_ref[g] = jnp.dot(
+            hidden[...], sparse[g], preferred_element_type=jnp.float32
+        ).astype(jnp.bfloat16)
+        pending.append(scatter(g, 0))
     teachers = []
     for g in range(groups):
         copy = pltpu.make_async_copy(
@@ -181,6 +219,10 @@
         )
         copy.start()
         teachers.append(copy)
+    turned_ref[...] = hidden[...].T
+    gate, up_sum, sig, act = activations(own_ref, peer_ref)
+    factors_ref[0] = up_sum * sig * (1.0 + gate * (1.0 - sig))
+    factors_ref[1] = act
 
     for s in range(bits):
         half = tokens >> (s + 1)
@@ -204,54 +246,41 @@
                 s = bits - 1 - t
                 here = out_ref.at[g, at(starts[g][s + 1], tokens >> (s + 1))]
                 pending[g] = send(g, bits + t, orders[g][s], here, here)
+            else:
+                share = contract_cols(out_ref[g], sparse[g])
+                if g == 0:
+                    gh_ref[...] = share
+                else:
+                    gh_ref[...] += share
+    gh_send_ref[...] = gh_ref[...].astype(jnp.bfloat16)
     for copy in copies:
         copy.wait_send()
 
 
-def down_kernel(res_ref, hidden_ref, wd_ref, md_ref, gd_ref, gh_ref, send_ref, turned):
-    k = pl.program_id(0)
-
-    @pl.when(k == 0)
-    def _():
-        turned[...] = hidden_ref[...].T
-
-    res = res_ref[0]
-    mask = md_ref[...]
-    gd = jnp.dot(turned[...], res, preferred_element_type=jnp.float32)
-    gd_ref[...] = masked(gd, mask).astype(jnp.bfloat16)
-    gh = contract_cols(res, masked(wd_ref[...], mask))
-
-    @pl.when(k == 0)
-    def _():
-        gh_ref[...] = gh
-
-    @pl.when(k > 0)
-    def _():
-        gh_ref[...] += gh
-
-    @pl.when(k == pl.num_programs(0) - 1)
-    def _():
-        send_ref[...] = gh_ref[...].astype(jnp.bfloat16)
+def down_kernel(turned_ref, res_ref, md_ref, gd_ref):
+    width = gd_ref.shape[1]
+    mask = widened(md_ref[...], pl.program_id(0) * (width // BLOCK), width)
+    total = jnp.dot(turned_ref[...], res_ref[0], preferred_element_type=jnp.float32)
+    gd_ref[...] = masked(total.astype(jnp.bfloat16), mask)
 
 
 def weights_kernel(
-    own_ref, peer_ref, gh_ref, gh_peer_ref, x_ref, mg_ref, mu_ref, gg_ref, gu_ref, grads
+    factors_ref, gh_ref, gh_peer_ref, x_ref, mg_ref, mu_ref, gg_ref, gu_ref, grads
 ):
     hidden = gg_ref.shape[1]
 
     @pl.when(pl.program_id(0) == 0)
     def _():
-        gate, up, sig, act = activations(own_ref, peer_ref)
         gh = gh_ref[...] + gh_peer_ref[...].astype(jnp.float32)
-        grads[:, :hidden] = (gh * up * sig * (1.0 + gate * (1.0 - sig))).astype(jnp.bfloat16)
-        grads[:, hidden:] = (gh * act).astype(jnp.bfloat16)
+        grads[:, :hidden] = (gh * factors_ref[0]).astype(jnp.bfloat16)
+        grads[:, hidden:] = (gh * factors_ref[1]).astype(jnp.bfloat16)
 
     turned = x_ref[...].T
     for i, (m_ref, out_ref) in enumerate(((mg_ref, gg_ref), (mu_ref, gu_ref))):
         total = jnp.dot(
             turned, grads[:, i * hidden : (i + 1) * hidden], preferred_element_type=jnp.float32
         )
-        out_ref[...] = masked(total, m_ref[...]).astype(jnp.bfloat16)
+        out_ref[...] = masked(total.astype(jnp.bfloat16), widened(m_ref[...], 0, hidden))
 
 
 def params(**more):
@@ -268,79 +297,85 @@
     tile = TILE
     steps = depth // tile
     f32, bf16 = jnp.float32, jnp.bfloat16
-    rows = tile // BLOCK
     shape = jax.ShapeDtypeStruct
-    wide_gate = jnp.repeat(mask_gate.astype(f32), BLOCK, axis=1)
-    wide_up = jnp.repeat(mask_up.astype(f32), BLOCK, axis=1)
-    wide_down = jnp.repeat(mask_down.astype(f32), BLOCK, axis=1)
-    x_spec = pl.BlockSpec((tokens, tile), lambda k: (0, k))
-    w_spec = pl.BlockSpec((tile, units), lambda k: (k, 0))
-    m_spec = pl.BlockSpec((rows, units), lambda k: (k, 0))
-    wd_spec = pl.BlockSpec((units, tile), lambda k: (0, k))
-    md_spec = pl.BlockSpec((units // BLOCK, tile), lambda k: (0, k))
-    part_spec = pl.BlockSpec((1, tokens, tile), lambda k: (k, 0, 0))
     both, one = (2, tokens, units), (tokens, units)
     product = 2 * tokens * depth * units
 
     def cost(products, moved):
         return pl.CostEstimate(flops=products * product, bytes_accessed=moved, transcendentals=0)
 
+    def specs(tile):
+        return (
+            pl.BlockSpec((tokens, tile), lambda k: (0, k)),
+            pl.BlockSpec((tile, units), lambda k: (k, 0)),
+            pl.BlockSpec((tile // BLOCK, units // BLOCK), lambda k: (k, 0)),
+        )
+
+    x_spec, w_spec, m_spec = specs(2 * tile)
     own, mine = pl.pallas_call(
         forward_kernel,
-        grid=(steps,),
+        grid=(steps // 2,),
         in_specs=[x_spec, w_spec, w_spec, m_spec, m_spec],
         out_specs=[whole(both), whole(both)],
         out_shape=[shape(both, f32), shape(both, bf16)],
         compiler_params=params(),
         cost_estimate=cost(2, 4 * depth * units),
-    )(hidden_in, w_gate, w_up, wide_gate, wide_up)
+    )(hidden_in, w_gate, w_up, mask_gate, mask_up)
     peer = lax.ppermute(mine, "tensor", [(0, 1), (1, 0)])
-    partial, hidden = pl.pallas_call(
-        student_kernel,
-        grid=(steps,),
-        in_specs=[whole(both), whole(both), wd_spec, md_spec],
-        out_specs=[part_spec, whole(one)],
-        out_shape=[shape((steps, tokens, tile), bf16), shape(one, bf16)],
-        compiler_params=params(),
-        cost_estimate=cost(1, 2 * depth * units),
-    )(own, peer, w_down, wide_down)
     bits = n.bit_length() - 1
-    residual = pl.pallas_call(
+    vmem = pl.BlockSpec(memory_space=pltpu.VMEM)
+    hbm = pl.BlockSpec(memory_space=pl.ANY)
+    groups = (steps, tokens, tile)
+    residual, turned, factors, gh, gh_mine = pl.pallas_call(
         functools.partial(residual_kernel, n),
-        in_specs=[pl.BlockSpec(memory_space=pltpu.VMEM), pl.BlockSpec(memory_space=pl.ANY)],
-        out_specs=pl.BlockSpec(memory_space=pltpu.VMEM),
-        out_shape=shape((steps, tokens, tile), bf16),
+        in_specs=[vmem, vmem, vmem, hbm, hbm],
+        out_specs=[vmem] * 5,
+        out_shape=[
+            shape(groups, bf16),
+            shape((units, tokens), bf16),
+            shape(both, f32),
+            shape(one, f32),
+            shape(one, bf16),
+        ],
         scratch_shapes=[
-            pltpu.VMEM((steps, tokens, tile), bf16),
-            pltpu.VMEM((steps, tokens, tile), bf16),
+            pltpu.VMEM(one, bf16),
+            pltpu.VMEM(groups, bf16),
+            pltpu.VMEM((steps, units, tile), bf16),
+            pltpu.VMEM(groups, bf16),
+            pltpu.VMEM(groups, bf16),
             pltpu.VMEM((steps, tokens // n, tile), bf16),
+            pltpu.SemaphoreType.DMA((steps,)),
             pltpu.SemaphoreType.DMA((steps,)),
             pltpu.SemaphoreType.DMA((steps, 2 * bits)),
             pltpu.SemaphoreType.DMA((steps, 2 * bits)),
         ],
         compiler_params=params(collective_id=0, has_side_effects=True),
-    )(partial, teacher)
-    grad_down, gh, gh_mine = pl.pallas_call(
+    )(own, peer, mask_down, w_down, teacher)
+    gh_peer = lax.ppermute(gh_mine, "tensor", [(0, 1), (1, 0)])
+    grad_down = pl.pallas_call(
         down_kernel,
         grid=(steps,),
-        in_specs=[part_spec, whole(one), wd_spec, md_spec],
-        out_specs=[wd_spec, whole(one), whole(one)],
-        out_shape=[shape((units, depth), bf16), shape(one, f32), shape(one, bf16)],
-        scratch_shapes=[pltpu.VMEM((units, tokens), bf16)],
+        in_specs=[
+            whole((units, tokens)),
+            pl.BlockSpec((1, tokens, tile), lambda k: (k, 0, 0)),
+            whole(mask_down.shape),
+        ],
+        out_specs=pl.BlockSpec((units, tile), lambda k: (0, k)),
+        out_shape=shape((units, depth), bf16),
         compiler_params=params(),
-        cost_estimate=cost(2, 4 * depth * units),
-    )(residual, hidden, w_down, wide_down)
-    gh_peer = lax.ppermute(gh_mine, "tensor", [(0, 1), (1, 0)])
+        cost_estimate=cost(1, 2 * depth * units),
+    )(turned, residual, mask_down)
+    x_spec, w_spec, m_spec = specs(tile)
     grad_gate, grad_up = pl.pallas_call(
         weights_kernel,
         grid=(steps,),
-        in_specs=[whole(both), whole(both), whole(one), whole(one), x_spec, m_spec, m_spec],
+        in_specs=[whole(both), whole(one), whole(one), x_spec, m_spec, m_spec],
         out_specs=[w_spec, w_spec],
         out_shape=[shape((depth, units), bf16)] * 2,
         scratch_shapes=[pltpu.VMEM((tokens, 2 * units), bf16)],
         compiler_params=params(),
         cost_estimate=cost(2, 4 * depth * units),
-    )(own, peer, gh, gh_peer, hidden_in, wide_gate, wide_up)
+    )(factors, gh, gh_peer, hidden_in, mask_gate, mask_up)
     return (grad_gate, grad_up, grad_down)
 
 
@@ -348,7 +383,7 @@
     tokens, depth = args[0].shape
     units = args[2].shape[1]
     fits = tensor == 2 and n >= 4 and n & (n - 1) == 0 and tokens % (16 * n) == 0
-    if fits and depth % TILE == 0 and units % 256 == 0:
+    if fits and depth % (2 * TILE) == 0 and units % 256 == 0:
         return with_kernels(n, *args)
     return plain(*args)
 

time: 168 us -> 152 us (0.905)
  Pallas kernels: 153 us -> 141 us
  waiting for transfers between devices: 5.75 us -> 4 us
    pallas_call x4 -> x3, Pallas kernels: 136 us -> 121 us  [the longest x1 92.8 us: with_kernels(): pl.pallas_call(functools.partial(residual_kernel, n), in_specs=[vmem, vme...]
    pallas_call x1, Pallas kernels: 16.9 us -> 19.8 us  [with_kernels(): pl.pallas_call(weights_kernel, grid=(steps,), in_specs=[whole(both), whol...]
    ppermute x1, waiting for transfers between devices: 2.86 us -> 0.01 us  [with_kernels(): gh_peer = lax.ppermute(gh_mine, 'tensor', [(0, 1), (1, 0)])]
    unnamed x6, local copies, waits for them, and re-layouts: 2.33 us -> 5.08 us
    reshape x3 -> x0, local copies, waits for them, and re-layouts: 2.7 us -> none  [the longest x1 0.9 us: with_kernels(): wide_down = jnp.repeat(mask_down.astype(f32), BLOCK, axis=1)]
  transfers between devices with their start and end apart: 2 -> 2, of which waited for: 2 -> 1; matrix products, arithmetic and copies ran while one was open for 1% -> 0% of each run, Pallas kernels for 0% -> 7%
where the time goes in v2:
time: 152 us
  Pallas kernels  141 us (93%)
  local copies, waits for them, and re-layouts  5.08 us (3%)
  waiting for transfers between devices  4 us (3%)
    pallas_call x1, Pallas kernels, with_kernels(): pl.pallas_call(functools.partial(residual_kernel, n), in_specs=[vmem, vme...  92.8 us
    pallas_call x1, Pallas kernels, with_kernels(): pl.pallas_call(weights_kernel, grid=(steps,), in_specs=[whole(both), whol...  19.8 us
    pallas_call x1, Pallas kernels, with_kernels(): pl.pallas_call(forward_kernel, grid=(steps // 2,), in_specs=[x_spec, w_sp...  18.2 us
    pallas_call x1, Pallas kernels, with_kernels(): pl.pallas_call(down_kernel, grid=(steps,), in_specs=[whole((units, tokens...  10.4 us
    unnamed x6, local copies, waits for them, and re-layouts  5.08 us
    ppermute x1, waiting for transfers between devices, with_kernels(): peer = lax.ppermute(mine, 'tensor', [(0, 1), (1, 0)])  4 us
  transfers between devices with their start and end apart: 2, of which 1 were waited for; matrix products, arithmetic and copies ran while one was open for 0% of the time, Pallas kernels for 7%

profile of v2, /device:TPU:0, one launch (start us, length us, event | category | flops | bytes accessed | tf_op | source)
XLA Modules:
  0.0 151.5 jit_solution(15329296070430079130)
XLA Ops:
  0.6 1.4 copy.11.mg_ref
  2.0 1.4 copy.12.mu_ref
  3.4 18.2 %shard_map.103 = (f32[2,512,1024]{2,1,0:T(8,128)}, bf16[2,512,1024]{2,1,0:T(8,128)(2,1)}) custom-call(bf16[512,4096]{1,0:T(8,128)(2,1)} %x_ref.3, bf16[4096,1024]{1,0:T(8,128)(2,1)} %wg_ref.1, bf16[4096,1024]{1,0:T(8,128)(2,1)} %wu_ref.1, s32[64,16]{1,0:T(8,128)} %copy.11.mg_ref, s32[64,16]{1,0:T(8,128)} %copy.12.mu_ref), custom_call_target="tpu_custom_call" | custom-call | flops 8589934592 | bytes 16777216 | tf_op jit(solution)/shard_map/pallas_call | solution.py:315
  21.6 0.5 collective-permute-start
  22.1 4.0 %collective-permute-done.peer_ref = bf16[2,512,1024]{2,1,0:T(8,128)(2,1)S(1)} collective-permute-done((bf16[2,512,1024]{2,1,0:T(8,128)(2,1)}, bf16[2,512,1024]{2,1,0:T(8,128)(2,1)S(1)}, u32[]{:S(2)}, u32[]{:S(2)}) %collective-permute-start) | collective-permute-done | bytes 2097184 | tf_op jit(solution)/shard_map/ppermute | solution.py:324
  26.1 0.0 copy-start
  26.1 1.3 copy-done
  27.4 92.8 %shard_map.104 = (bf16[8,512,512]{2,1,0:T(8,128)(2,1)}, bf16[1024,512]{1,0:T(8,128)(2,1)}, f32[2,512,1024]{2,1,0:T(8,128)}, f32[512,1024]{1,0:T(8,128)}, bf16[512,1024]{1,0:T(8,128)(2,1)}) custom-call(f32[2,512,1024]{2,1,0:T(8,128)} %get-tuple-element.12.own_ref, bf16[2,512,1024]{2,1,0:T(8,128)(2,1)} %copy-done, s32[16,64]{1,0:T(8,128)} %md_ref.3, ...), custom_call_target="tpu_custom_call" | custom-call | tf_op jit(solution)/shard_map/pallas_call | solution.py:329
  120.2 0.1 collective-permute-start.1
  120.3 10.4 %shard_map.106 = bf16[1024,4096]{1,0:T(8,128)(2,1)} custom-call(bf16[1024,512]{1,0:T(8,128)(2,1)} %get-tuple-element.19.turned_ref, bf16[8,512,512]{2,1,0:T(8,128)(2,1)} %get-tuple-element.20.res_ref, s32[16,64]{1,0:T(8,128)} %md_ref.3), custom_call_target="tpu_custom_call" | custom-call | flops 4294967296 | bytes 8388608 | tf_op jit(solution)/shard_map/pallas_call | solution.py:355
  130.7 0.0 collective-permute-done.1.gh_peer_ref
  130.7 0.0 copy-start.1
  130.7 1.0 copy-done.1
  131.7 19.8 %shard_map.105 = (bf16[4096,1024]{1,0:T(8,128)(2,1)}, bf16[4096,1024]{1,0:T(8,128)(2,1)}) custom-call(f32[2,512,1024]{2,1,0:T(8,128)} %get-tuple-element.14.factors_ref, f32[512,1024]{1,0:T(8,128)} %get-tuple-element.15.gh_ref, bf16[512,1024]{1,0:T(8,128)(2,1)} %copy-done.1, bf16[512,4096]{1,0:T(8,128)(2,1)} %x_ref.3, s32[64,16]{1,0:T(8,128)} %copy.11.mg_ref, ...), custom_call_target="tpu_custom_call" | custom-call | flops 8589934592 | bytes 16777216 | tf_op jit(solution)/shard_map/pallas_call | solution.py:369
Async XLA Ops:
  21.6 4.4 %collective-permute-start = (bf16[2,512,1024]{2,1,0:T(8,128)(2,1)}, bf16[2,512,1024]{2,1,0:T(8,128)(2,1)S(1)}, u32[]{:S(2)}, u32[]{:S(2)}) collective-permute-start(bf16[2,512,1024]{2,1,0:T(8,128)(2,1)} %get-tuple-element.13), channel_id=1, source_target_pairs={{0,1},{1,0},{2,3},{3,2},{4,5},{5,4},{6,7},{7,6},{8,9},{9,8},{10,11... | collective-permute-start | bytes 6291464 | tf_op jit(solution)/shard_map/ppermute | solution.py:324
  26.1 1.3 copy-start
  120.2 10.5 %collective-permute-start.1 = (bf16[512,1024]{1,0:T(8,128)(2,1)}, bf16[512,1024]{1,0:T(8,128)(2,1)S(1)}, u32[]{:S(2)}, u32[]{:S(2)}) collective-permute-start(bf16[512,1024]{1,0:T(8,128)(2,1)} %get-tuple-element.16), channel_id=1, source_target_pairs={{0,1},{1,0},{2,3},{3,2},{4,5},{5,4},{6,7},{7,6},{8,9},{9,8},{10,11... | collective-permute-start | bytes 3145736 | tf_op jit(solution)/shard_map/ppermute | solution.py:354
  130.7 1.0 copy-start.1

commit v3 on v2

--- a/solution.py
+++ b/solution.py
@@ -265,7 +265,7 @@
 
 
 def weights_kernel(
-    factors_ref, gh_ref, gh_peer_ref, x_ref, mg_ref, mu_ref, gg_ref, gu_ref, grads
+    factors_ref, gh_ref, gh_peer_ref, x_ref, mg_ref, mu_ref, gg_ref, gu_ref, grads, keep
 ):
     hidden = gg_ref.shape[1]
 
@@ -273,14 +273,18 @@
     def _():
         gh = gh_ref[...] + gh_peer_ref[...].astype(jnp.float32)
         grads[:, :hidden] = (gh * factors_ref[0]).astype(jnp.bfloat16)
+        keep[0] = widened(mg_ref[...], 0, hidden)
+        keep[1] = widened(mu_ref[...], 0, hidden)
         grads[:, hidden:] = (gh * factors_ref[1]).astype(jnp.bfloat16)
 
     turned = x_ref[...].T
-    for i, (m_ref, out_ref) in enumerate(((mg_ref, gg_ref), (mu_ref, gu_ref))):
+    rows = gg_ref.shape[0] // BLOCK
+    first = pl.multiple_of(pl.program_id(0) * rows, rows)
+    for i, out_ref in enumerate((gg_ref, gu_ref)):
         total = jnp.dot(
             turned, grads[:, i * hidden : (i + 1) * hidden], preferred_element_type=jnp.float32
         )
-        out_ref[...] = masked(total.astype(jnp.bfloat16), widened(m_ref[...], 0, hidden))
+        out_ref[...] = masked(total, keep[i, pl.ds(first, rows)]).astype(jnp.bfloat16)
 
 
 def params(**more):
@@ -365,14 +369,19 @@
         compiler_params=params(),
         cost_estimate=cost(1, 2 * depth * units),
     )(turned, residual, mask_down)
-    x_spec, w_spec, m_spec = specs(tile)
+    x_spec, w_spec, _ = specs(tile)
+    m_spec = whole(mask_gate.shape)
+    wide = (depth // BLOCK, units)
     grad_gate, grad_up = pl.pallas_call(
         weights_kernel,
         grid=(steps,),
         in_specs=[whole(both), whole(one), whole(one), x_spec, m_spec, m_spec],
         out_specs=[w_spec, w_spec],
         out_shape=[shape((depth, units), bf16)] * 2,
-        scratch_shapes=[pltpu.VMEM((tokens, 2 * units), bf16)],
+        scratch_shapes=[
+            pltpu.VMEM((tokens, 2 * units), bf16),
+            pltpu.VMEM((2, *wide), f32),
+        ],
         compiler_params=params(),
         cost_estimate=cost(2, 4 * depth * units),
     )(factors, gh, gh_peer, hidden_in, mask_gate, mask_up)

time: 152 us -> 148 us (0.974)
  Pallas kernels: 141 us -> 137 us
    pallas_call x1, Pallas kernels: 19.8 us -> 16 us  [with_kernels(): pl.pallas_call(weights_kernel, grid=(steps,), in_specs=[whole(both), whol...]
where the time goes in v3:
time: 148 us
  Pallas kernels  137 us (93%)
  local copies, waits for them, and re-layouts  5.08 us (3%)
  waiting for transfers between devices  4 us (3%)
    pallas_call x1, Pallas kernels, with_kernels(): pl.pallas_call(functools.partial(residual_kernel, n), in_specs=[vmem, vme...  92.8 us
    pallas_call x1, Pallas kernels, with_kernels(): pl.pallas_call(forward_kernel, grid=(steps // 2,), in_specs=[x_spec, w_sp...  18.2 us
    pallas_call x1, Pallas kernels, with_kernels(): pl.pallas_call(weights_kernel, grid=(steps,), in_specs=[whole(both), whol...  16 us
    pallas_call x1, Pallas kernels, with_kernels(): pl.pallas_call(down_kernel, grid=(steps,), in_specs=[whole((units, tokens...  10.4 us
    unnamed x6, local copies, waits for them, and re-layouts  5.08 us
    ppermute x1, waiting for transfers between devices, with_kernels(): peer = lax.ppermute(mine, 'tensor', [(0, 1), (1, 0)])  4 us
  transfers between devices with their start and end apart: 2, of which 1 were waited for; matrix products, arithmetic and copies ran while one was open for 0% of the time, Pallas kernels for 7%

profile of v3, /device:TPU:0, one launch (start us, length us, event | category | flops | bytes accessed | tf_op | source)
XLA Modules:
  0.0 147.7 jit_solution(5074584376280465811)
XLA Ops:
  0.6 1.4 copy.11.mg_ref
  2.0 1.4 copy.12.mu_ref
  3.4 18.2 %shard_map.103 = (f32[2,512,1024]{2,1,0:T(8,128)}, bf16[2,512,1024]{2,1,0:T(8,128)(2,1)}) custom-call(bf16[512,4096]{1,0:T(8,128)(2,1)} %x_ref.3, bf16[4096,1024]{1,0:T(8,128)(2,1)} %wg_ref.1, bf16[4096,1024]{1,0:T(8,128)(2,1)} %wu_ref.1, s32[64,16]{1,0:T(8,128)} %copy.11.mg_ref, s32[64,16]{1,0:T(8,128)} %copy.12.mu_ref), custom_call_target="tpu_custom_call" | custom-call | flops 8589934592 | bytes 16777216 | tf_op jit(solution)/shard_map/pallas_call | solution.py:319
  21.6 0.5 collective-permute-start
  22.1 4.0 %collective-permute-done.peer_ref = bf16[2,512,1024]{2,1,0:T(8,128)(2,1)S(1)} collective-permute-done((bf16[2,512,1024]{2,1,0:T(8,128)(2,1)}, bf16[2,512,1024]{2,1,0:T(8,128)(2,1)S(1)}, u32[]{:S(2)}, u32[]{:S(2)}) %collective-permute-start) | collective-permute-done | bytes 2097184 | tf_op jit(solution)/shard_map/ppermute | solution.py:328
  26.1 0.0 copy-start
  26.1 1.3 copy-done
  27.4 92.8 %shard_map.104 = (bf16[8,512,512]{2,1,0:T(8,128)(2,1)}, bf16[1024,512]{1,0:T(8,128)(2,1)}, f32[2,512,1024]{2,1,0:T(8,128)}, f32[512,1024]{1,0:T(8,128)}, bf16[512,1024]{1,0:T(8,128)(2,1)}) custom-call(f32[2,512,1024]{2,1,0:T(8,128)} %get-tuple-element.12.own_ref, bf16[2,512,1024]{2,1,0:T(8,128)(2,1)} %copy-done, s32[16,64]{1,0:T(8,128)} %md_ref.3, ...), custom_call_target="tpu_custom_call" | custom-call | tf_op jit(solution)/shard_map/pallas_call | solution.py:333
  120.2 0.1 collective-permute-start.1
  120.3 10.4 %shard_map.106 = bf16[1024,4096]{1,0:T(8,128)(2,1)} custom-call(bf16[1024,512]{1,0:T(8,128)(2,1)} %get-tuple-element.19.turned_ref, bf16[8,512,512]{2,1,0:T(8,128)(2,1)} %get-tuple-element.20.res_ref, s32[16,64]{1,0:T(8,128)} %md_ref.3), custom_call_target="tpu_custom_call" | custom-call | flops 4294967296 | bytes 8388608 | tf_op jit(solution)/shard_map/pallas_call | solution.py:359
  130.7 0.0 collective-permute-done.1.gh_peer_ref
  130.7 0.0 copy-start.1
  130.7 1.0 copy-done.1
  131.7 16.0 %shard_map.105 = (bf16[4096,1024]{1,0:T(8,128)(2,1)}, bf16[4096,1024]{1,0:T(8,128)(2,1)}) custom-call(f32[2,512,1024]{2,1,0:T(8,128)} %get-tuple-element.14.factors_ref, f32[512,1024]{1,0:T(8,128)} %get-tuple-element.15.gh_ref, bf16[512,1024]{1,0:T(8,128)(2,1)} %copy-done.1, bf16[512,4096]{1,0:T(8,128)(2,1)} %x_ref.3, s32[64,16]{1,0:T(8,128)} %copy.11.mg_ref, ...), custom_call_target="tpu_custom_call" | custom-call | flops 8589934592 | bytes 16777216 | tf_op jit(solution)/shard_map/pallas_call | solution.py:375
Async XLA Ops:
  21.6 4.4 %collective-permute-start = (bf16[2,512,1024]{2,1,0:T(8,128)(2,1)}, bf16[2,512,1024]{2,1,0:T(8,128)(2,1)S(1)}, u32[]{:S(2)}, u32[]{:S(2)}) collective-permute-start(bf16[2,512,1024]{2,1,0:T(8,128)(2,1)} %get-tuple-element.13), channel_id=1, source_target_pairs={{0,1},{1,0},{2,3},{3,2},{4,5},{5,4},{6,7},{7,6},{8,9},{9,8},{10,11... | collective-permute-start | bytes 6291464 | tf_op jit(solution)/shard_map/ppermute | solution.py:328
  26.1 1.3 copy-start
  120.2 10.5 %collective-permute-start.1 = (bf16[512,1024]{1,0:T(8,128)(2,1)}, bf16[512,1024]{1,0:T(8,128)(2,1)S(1)}, u32[]{:S(2)}, u32[]{:S(2)}) collective-permute-start(bf16[512,1024]{1,0:T(8,128)(2,1)} %get-tuple-element.16), channel_id=1, source_target_pairs={{0,1},{1,0},{2,3},{3,2},{4,5},{5,4},{6,7},{7,6},{8,9},{9,8},{10,11... | collective-permute-start | bytes 3145736 | tf_op jit(solution)/shard_map/ppermute | solution.py:358
  130.7 1.0 copy-start.1
